TPU v7x, 256 devices: a whole 4x4x8 slice. The times are simulated.
256 devices in a mesh: view: 8 (over z), wide: 32 (over y, x, core).
Axes of the slice: x: 4, y: 4, z: 8, core: 2. Of those that a mesh axis runs over, the one named last changes fastest.
Arguments:
- tracer: float32 [512, 1024, 128], P('view', 'wide'), may hold values from 0.05 to 5
- velocity: float32 [3, 512, 1024, 128], P(None, 'view', 'wide'), may hold values from -0.15 to 0.15
- buildings: int32 [512, 1024, 128], P('view', 'wide'), may hold values from 0 to 1, as said below
- source: float32 [512, 1024, 128], P('view', 'wide'), may hold values from 0 to 0.5
Outputs:
- tracer_next: float32 [512, 1024, 128], P('view', 'wide')
- picture: float32 [4, 1024, 128], P(None, 'wide', 'view')
Inputs may be any that keep to these rules, and one draw needn't show every extreme that they name: `buildings`: each column of cells at a fixed first and second index is inside a building from the ground up to some height of at most 64 cells, and outside above it.
All inputs are finite; a program needn't handle non-finite values.
Results may differ from a plain program's by a relative error of at most 0.000056.
Values sent between devices are 32-bit elements; how exact they have to be, the bound alone decides.
A program may use at most 64 MiB of HBM per device.

v0:
```python
import jax
import jax.numpy as jnp
from jax import lax
from jax.sharding import PartitionSpec as P

STEPS = 4


def padded_2(cells, sides, width):
    for axis, dim in sides:
        count = lax.axis_size(axis)
        head = lax.slice_in_dim(cells, 0, width, axis=dim)
        tail = lax.slice_in_dim(cells, cells.shape[dim] - width, cells.shape[dim], axis=dim)
        cells = jnp.concatenate(
            [
                lax.ppermute(tail, axis, [(i, (i + 1) % count) for i in range(count)]),
                cells,
                lax.ppermute(head, axis, [((i + 1) % count, i) for i in range(count)]),
            ],
            axis=dim,
        )
    return cells


def advance(tracer, velocity, open_cells, source):
    face_zero = velocity[0][:-1] * open_cells[:-1] * open_cells[1:]
    flux_zero = jnp.maximum(face_zero, 0.0) * tracer[:-1] + jnp.minimum(face_zero, 0.0) * tracer[1:]
    delta_zero = (flux_zero[1:] - flux_zero[:-1])[:, 1:-1]
    face_one = velocity[1][:, :-1] * open_cells[:, :-1] * open_cells[:, 1:]
    flux_one = (
        jnp.maximum(face_one, 0.0) * tracer[:, :-1] + jnp.minimum(face_one, 0.0) * tracer[:, 1:]
    )
    delta_one = (flux_one[:, 1:] - flux_one[:, :-1])[1:-1]
    face_two = velocity[2][:, :, :-1] * open_cells[:, :, :-1] * open_cells[:, :, 1:]
    flux_two = (
        jnp.maximum(face_two, 0.0) * tracer[:, :, :-1]
        + jnp.minimum(face_two, 0.0) * tracer[:, :, 1:]
    )
    padded = jnp.pad(flux_two, ((0, 0), (0, 0), (1, 1)))
    delta_two = (padded[:, :, 1:] - padded[:, :, :-1])[1:-1, 1:-1]
    inner_tracer = tracer[1:-1, 1:-1]
    return open_cells[1:-1, 1:-1] * (
        inner_tracer - delta_zero - delta_one - delta_two + source[1:-1, 1:-1]
    )


def shade_cells(tracer, open_cells):
    shading = tracer / (1.0 + tracer)
    walls = 1.0 - open_cells
    red = open_cells * shading + 0.55 * walls
    green = open_cells * jnp.exp(-0.5 * tracer) + 0.5 * walls
    blue = open_cells * (0.2 + 0.6 * shading * shading) + 0.45 * walls
    return (red, green, blue)


def composite(nearer, farther):
    colors = nearer[:3] + nearer[3:] * farther[:3]
    return jnp.concatenate([colors, nearer[3:] * farther[3:]], axis=0)


def fold_in_order(layers):
    start_value = jnp.concatenate(
        [
            jnp.zeros((3,) + layers.shape[2:], jnp.float32),
            jnp.ones((1,) + layers.shape[2:], jnp.float32),
        ],
        axis=0,
    )

    def fold_step(running, layer_piece):
        return (composite(running, layer_piece), None)

    result, unused = lax.scan(fold_step, start_value, layers)
    return result


def finish_pixels(result):
    return jnp.concatenate([result[:3], 1.0 - result[3:]], axis=0)


def march_steps(tracer, speeds, open_wide, source_wide):
    current = tracer
    for substep in range(STEPS):
        tracer_wide = padded_2(current, (("view", 0), ("wide", 1)), 1)
        current = advance(tracer_wide, speeds, open_wide, source_wide)
    return current


def on_device(tracer, velocity, buildings, source):
    open_cells = (1 - buildings).astype(jnp.float32)
    static = jnp.concatenate([velocity, open_cells[None], source[None]], axis=0)
    grown_static = padded_2(static, (("view", 1), ("wide", 2)), 1)
    current = march_steps(tracer, grown_static[:3], grown_static[3], grown_static[4])
    view_count = lax.axis_size("view")
    depth_cells = float(tracer.shape[0] * view_count)
    extinction = (current * open_cells + 4.0 * (1.0 - open_cells)) / depth_cells
    before = jnp.cumsum(extinction, axis=0) - extinction
    weight = jnp.exp(-before) * (1.0 - jnp.exp(-extinction))
    red, green, blue = shade_cells(current, open_cells)
    partial_value = jnp.stack(
        [
            jnp.sum(weight * red, axis=0),
            jnp.sum(weight * green, axis=0),
            jnp.sum(weight * blue, axis=0),
            jnp.exp(-jnp.sum(extinction, axis=0)),
        ]
    )
    height = partial_value.shape[2]
    block_width = height // view_count
    position = lax.axis_index("view")
    pieces = lax.all_gather(partial_value[None], "view", axis=0, tiled=True)
    mine = lax.dynamic_slice_in_dim(pieces, position * block_width, block_width, 3)
    picture = finish_pixels(fold_in_order(mine))
    return (current, picture)


def solution(mesh):
    return jax.shard_map(
        on_device,
        mesh=mesh,
        in_specs=(
            P("view", "wide", None),
            P(None, "view", "wide", None),
            P("view", "wide", None),
            P("view", "wide", None),
        ),
        out_specs=(P("view", "wide", None), P(None, "wide", "view")),
        check_vma=False,
    )
```

profile of v0, /device:TPU:32, one launch (start us, length us, event | category | flops | bytes accessed | tf_op | source)
XLA Modules:
  0.0 111.1 jit_solution(14347198532158714569)
XLA Ops:
  0.6 0.8 fusion.57
  1.5 1.8 %collective-permute-start.5 = (f32[1,32,128]{2,1,0:T(8,128)S(1)}, f32[1,32,128]{2,1,0:T(8,128)S(1)}, u32[]{:S(2)}, u32[]{:S(2)}) collective-permute-start(f32[1,32,128]{2,1,0:T(8,128)S(1)} %get-tuple-element.84), channel_id=1, source_target_pairs={{32,0},{64,32},{96,64},{128,96},{160,128},{192,160},{224,192},{0,2... | collective-permute-start | bytes 49160 | tf_op jit(solution)/shard_map/ppermute | solution.py:18
  3.5 1.3 %convert_bitcast_fusion = f32[1,64,32,128]{3,2,1,0:T(8,128)S(1)} fusion(s32[64,32,128]{2,1,0:T(8,128)} %param.8), kind=kLoop, calls=%fused_computation.110 | loop fusion | flops 524288 | bytes 2097152 | tf_op jit(solution)/shard_map/broadcast_in_dim | solution.py:91
  4.9 1.0 pad_maximum_fusion.13
  5.9 2.0 %collective-permute-start = (f32[5,1,32,128]{3,2,1,0:T(8,128)S(1)}, f32[5,1,32,128]{3,2,1,0:T(8,128)S(1)}, u32[]{:S(2)}, u32[]{:S(2)}) collective-permute-start(f32[5,1,32,128]{3,2,1,0:T(8,128)S(1)} %get-tuple-element.44), channel_id=1, source_target_pairs={{0,32},{32,64},{64,96},{96,128},{128,160},{160,192},{192,224},{224... | collective-permute-start | bytes 245768 | tf_op jit(solution)/shard_map/ppermute | solution.py:16
  7.9 2.1 %collective-permute-start.1 = (f32[5,1,32,128]{3,2,1,0:T(8,128)S(1)}, f32[5,1,32,128]{3,2,1,0:T(8,128)S(1)}, u32[]{:S(2)}, u32[]{:S(2)}) collective-permute-start(f32[5,1,32,128]{3,2,1,0:T(8,128)S(1)} %get-tuple-element.45), channel_id=1, source_target_pairs={{32,0},{64,32},{96,64},{128,96},{160,128},{192,160},{224,192},{0,2... | collective-permute-start | bytes 245768 | tf_op jit(solution)/shard_map/ppermute | solution.py:18
  10.2 5.1 %collective-permute-start.7 = (f32[66,1,128]{2,1,0:T(1,128)S(1)}, f32[66,1,128]{2,1,0:T(1,128)S(1)}, u32[]{:S(2)}, u32[]{:S(2)}) collective-permute-start(f32[66,1,128]{2,1,0:T(1,128)S(1)} %get-tuple-element.77), channel_id=1, source_target_pairs={{1,0},{2,1},{3,2},{4,3},{5,4},{6,5},{7,6},{8,7},{9,8},{10,9},{11,1... | collective-permute-start | bytes 101384 | tf_op jit(solution)/shard_map/ppermute | solution.py:18
  15.3 0.2 pad_maximum_fusion.10
  15.6 5.1 %collective-permute-start.3 = (f32[5,66,1,128]{3,2,1,0:T(1,128)S(1)}, f32[5,66,1,128]{3,2,1,0:T(1,128)S(1)}, u32[]{:S(2)}, u32[]{:S(2)}) collective-permute-start(f32[5,66,1,128]{3,2,1,0:T(1,128)S(1)} %get-tuple-element.43), channel_id=1, source_target_pairs={{1,0},{2,1},{3,2},{4,3},{5,4},{6,5},{7,6},{8,7},{9,8},{10,9},{11,1... | collective-permute-start | bytes 506888 | tf_op jit(solution)/shard_map/ppermute | solution.py:18
  20.7 0.2 pad_maximum_fusion.2
  20.9 2.8 %collective-permute-done.2 = f32[5,66,1,128]{3,2,1,0:T(1,128)S(1)} collective-permute-done((f32[5,66,1,128]{3,2,1,0:T(1,128)S(1)}, f32[5,66,1,128]{3,2,1,0:T(1,128)S(1)}, u32[]{:S(2)}, u32[]{:S(2)}) %collective-permute-start.2) | collective-permute-done | bytes 168992 | tf_op jit(solution)/shard_map/ppermute | solution.py:16
  23.7 2.7 %pad_maximum_fusion.1 = f32[5,66,34,128]{3,2,1,0:T(8,128)S(1)} fusion(f32[5,66,1,128]{3,2,1,0:T(1,128)S(1)} %collective-permute-done.3, f32[5,1,32,128]{3,2,1,0:T(8,128)S(1)} %collective-permute-done.1, f32[1,64,32,128]{3,2,1,0:T(8,128)S(1)} %bitcast.45, f32[1,64,32,128]{3,2,1,0:T(8,128)S(1)} %convert_bitcast_fusion, f32[3,64,32,128]{3,2,1,0:T(8,128)S(1)} %copy-done, ...), kind=kLoop, calls=%fused_computation.7 | loop fusion | flops 8616960 | bytes 11489280 | tf_op jit(solution)/shard_map/concatenate | solution.py:14
  26.5 0.4 slice_bitcast_fusion.1
  26.9 0.3 fusion.14
  27.2 0.5 fusion.7
  27.8 0.2 fusion.48
  28.2 0.8 fusion.6
  29.0 0.4 pad_slice_fusion.7
  29.5 0.9 fusion.37
  30.4 1.3 %collective-permute-start.8 = (f32[1,32,128]{2,1,0:T(8,128)S(1)}, f32[1,32,128]{2,1,0:T(8,128)S(1)}, u32[]{:S(2)}, u32[]{:S(2)}) collective-permute-start(f32[1,32,128]{2,1,0:T(8,128)S(1)} %get-tuple-element.82), channel_id=1, source_target_pairs={{0,32},{32,64},{64,96},{96,128},{128,160},{160,192},{192,224},{224... | collective-permute-start | bytes 49160 | tf_op jit(solution)/shard_map/ppermute | solution.py:16
  31.7 2.3 %collective-permute-start.9 = (f32[1,32,128]{2,1,0:T(8,128)S(1)}, f32[1,32,128]{2,1,0:T(8,128)S(1)}, u32[]{:S(2)}, u32[]{:S(2)}) collective-permute-start(f32[1,32,128]{2,1,0:T(8,128)S(1)} %get-tuple-element.83), channel_id=1, source_target_pairs={{32,0},{64,32},{96,64},{128,96},{160,128},{192,160},{224,192},{0,2... | collective-permute-start | bytes 49160 | tf_op jit(solution)/shard_map/ppermute | solution.py:18
  34.0 1.6 %collective-permute-done.8 = f32[1,32,128]{2,1,0:T(8,128)S(1)} collective-permute-done((f32[1,32,128]{2,1,0:T(8,128)S(1)}, f32[1,32,128]{2,1,0:T(8,128)S(1)}, u32[]{:S(2)}, u32[]{:S(2)}) %collective-permute-start.8) | collective-permute-done | bytes 16416 | tf_op jit(solution)/shard_map/ppermute | solution.py:16
  35.7 5.1 %collective-permute-start.11 = (f32[66,1,128]{2,1,0:T(1,128)S(1)}, f32[66,1,128]{2,1,0:T(1,128)S(1)}, u32[]{:S(2)}, u32[]{:S(2)}) collective-permute-start(f32[66,1,128]{2,1,0:T(1,128)S(1)} %get-tuple-element.75), channel_id=1, source_target_pairs={{1,0},{2,1},{3,2},{4,3},{5,4},{6,5},{7,6},{8,7},{9,8},{10,9},{11,1... | collective-permute-start | bytes 101384 | tf_op jit(solution)/shard_map/ppermute | solution.py:18
  40.8 1.6 %collective-permute-done.10 = f32[66,1,128]{2,1,0:T(1,128)S(1)} collective-permute-done((f32[66,1,128]{2,1,0:T(1,128)S(1)}, f32[66,1,128]{2,1,0:T(1,128)S(1)}, u32[]{:S(2)}, u32[]{:S(2)}) %collective-permute-start.10) | collective-permute-done | bytes 33824 | tf_op jit(solution)/shard_map/ppermute | solution.py:16
  42.4 0.3 fusion.8
  42.8 0.2 fusion.47
  43.0 0.2 pad_maximum_fusion.3
  43.2 0.3 fusion.13
  43.5 0.5 fusion.5
  44.1 0.4 pad_slice_fusion.5
  44.6 1.1 %fusion.32 = f32[64,32,128]{2,1,0:T(8,128)S(1)} fusion(f32[66,34,128]{2,1,0:T(8,128)S(1)} %get-tuple-element.57, f32[66,34,128]{2,1,0:T(8,128)S(1)} %get-tuple-element.56, f32[66,32,128]{2,1,0:T(8,128)S(1)} %get-tuple-element.55, f32[66,32,128]{2,1,0:T(8,128)S(1)} %get-tuple-element.54, f32[64,32,128]{2,1,0:T(8,128)S(1)} %fusion.37, ...), kind=kLoop, calls=%fused_computation.92 | loop fusion | flops 2097152 | bytes 10485760 | tf_op jit(solution)/shard_map/mul | solution.py:42
  45.7 3.0 %collective-permute-start.12 = (f32[1,32,128]{2,1,0:T(8,128)S(1)}, f32[1,32,128]{2,1,0:T(8,128)S(1)}, u32[]{:S(2)}, u32[]{:S(2)}) collective-permute-start(f32[1,32,128]{2,1,0:T(8,128)S(1)} %get-tuple-element.80), channel_id=1, source_target_pairs={{0,32},{32,64},{64,96},{96,128},{128,160},{160,192},{192,224},{224... | collective-permute-start | bytes 49160 | tf_op jit(solution)/shard_map/ppermute | solution.py:16
  48.7 0.4 collective-permute-start.13
  49.1 1.6 %collective-permute-done.12 = f32[1,32,128]{2,1,0:T(8,128)S(1)} collective-permute-done((f32[1,32,128]{2,1,0:T(8,128)S(1)}, f32[1,32,128]{2,1,0:T(8,128)S(1)}, u32[]{:S(2)}, u32[]{:S(2)}) %collective-permute-start.12) | collective-permute-done | bytes 16416 | tf_op jit(solution)/shard_map/ppermute | solution.py:16
  50.7 2.9 %collective-permute-done.13 = f32[1,32,128]{2,1,0:T(8,128)S(1)} collective-permute-done((f32[1,32,128]{2,1,0:T(8,128)S(1)}, f32[1,32,128]{2,1,0:T(8,128)S(1)}, u32[]{:S(2)}, u32[]{:S(2)}) %collective-permute-start.13) | collective-permute-done | bytes 16416 | tf_op jit(solution)/shard_map/ppermute | solution.py:18
  53.8 5.1 %collective-permute-start.15 = (f32[66,1,128]{2,1,0:T(1,128)S(1)}, f32[66,1,128]{2,1,0:T(1,128)S(1)}, u32[]{:S(2)}, u32[]{:S(2)}) collective-permute-start(f32[66,1,128]{2,1,0:T(1,128)S(1)} %get-tuple-element.73), channel_id=1, source_target_pairs={{1,0},{2,1},{3,2},{4,3},{5,4},{6,5},{7,6},{8,7},{9,8},{10,9},{11,1... | collective-permute-start | bytes 101384 | tf_op jit(solution)/shard_map/ppermute | solution.py:18
  58.8 1.6 %collective-permute-done.14 = f32[66,1,128]{2,1,0:T(1,128)S(1)} collective-permute-done((f32[66,1,128]{2,1,0:T(1,128)S(1)}, f32[66,1,128]{2,1,0:T(1,128)S(1)}, u32[]{:S(2)}, u32[]{:S(2)}) %collective-permute-start.14) | collective-permute-done | bytes 33824 | tf_op jit(solution)/shard_map/ppermute | solution.py:16
  60.4 0.2 pad_maximum_fusion.4
  60.7 0.3 fusion.12
  61.0 0.5 fusion.4
  61.4 0.3 fusion.9
  61.8 0.2 fusion.46
  62.2 0.4 pad_slice_fusion.3
  62.7 1.2 %fusion.27 = f32[64,32,128]{2,1,0:T(8,128)S(1)} fusion(f32[66,34,128]{2,1,0:T(8,128)S(1)} %get-tuple-element.53, f32[66,34,128]{2,1,0:T(8,128)S(1)} %get-tuple-element.52, f32[66,32,128]{2,1,0:T(8,128)S(1)} %get-tuple-element.51, f32[66,32,128]{2,1,0:T(8,128)S(1)} %get-tuple-element.50, f32[64,32,128]{2,1,0:T(8,128)S(1)} %fusion.32, ...), kind=kLoop, calls=%fused_computation.84 | loop fusion | flops 2097152 | bytes 10485760 | tf_op jit(solution)/shard_map/mul | solution.py:42
  63.9 2.1 %collective-permute-start.16 = (f32[1,32,128]{2,1,0:T(8,128)S(1)}, f32[1,32,128]{2,1,0:T(8,128)S(1)}, u32[]{:S(2)}, u32[]{:S(2)}) collective-permute-start(f32[1,32,128]{2,1,0:T(8,128)S(1)} %get-tuple-element.78), channel_id=1, source_target_pairs={{0,32},{32,64},{64,96},{96,128},{128,160},{160,192},{192,224},{224... | collective-permute-start | bytes 49160 | tf_op jit(solution)/shard_map/ppermute | solution.py:16
  66.0 1.7 %collective-permute-done.16 = f32[1,32,128]{2,1,0:T(8,128)S(1)} collective-permute-done((f32[1,32,128]{2,1,0:T(8,128)S(1)}, f32[1,32,128]{2,1,0:T(8,128)S(1)}, u32[]{:S(2)}, u32[]{:S(2)}) %collective-permute-start.16) | collective-permute-done | bytes 16416 | tf_op jit(solution)/shard_map/ppermute | solution.py:16
  67.7 2.0 %collective-permute-done.17 = f32[1,32,128]{2,1,0:T(8,128)S(1)} collective-permute-done((f32[1,32,128]{2,1,0:T(8,128)S(1)}, f32[1,32,128]{2,1,0:T(8,128)S(1)}, u32[]{:S(2)}, u32[]{:S(2)}) %collective-permute-start.17) | collective-permute-done | bytes 16416 | tf_op jit(solution)/shard_map/ppermute | solution.py:18
  69.8 5.1 %collective-permute-start.19 = (f32[66,1,128]{2,1,0:T(1,128)S(1)}, f32[66,1,128]{2,1,0:T(1,128)S(1)}, u32[]{:S(2)}, u32[]{:S(2)}) collective-permute-start(f32[66,1,128]{2,1,0:T(1,128)S(1)} %get-tuple-element.71), channel_id=1, source_target_pairs={{1,0},{2,1},{3,2},{4,3},{5,4},{6,5},{7,6},{8,7},{9,8},{10,9},{11,1... | collective-permute-start | bytes 101384 | tf_op jit(solution)/shard_map/ppermute | solution.py:18
  74.9 1.6 %collective-permute-done.18 = f32[66,1,128]{2,1,0:T(1,128)S(1)} collective-permute-done((f32[66,1,128]{2,1,0:T(1,128)S(1)}, f32[66,1,128]{2,1,0:T(1,128)S(1)}, u32[]{:S(2)}, u32[]{:S(2)}) %collective-permute-start.18) | collective-permute-done | bytes 33824 | tf_op jit(solution)/shard_map/ppermute | solution.py:16
  76.5 0.2 pad_maximum_fusion.5
  76.7 0.3 fusion.11
  77.0 1.0 copy-done.6
  78.1 0.4 fusion.3
  78.5 0.9 copy-done.4
  79.4 0.4 fusion.10
  79.8 0.2 fusion.45
  80.2 0.4 pad_slice_fusion.1
  80.6 0.9 copy-done.2
  81.5 1.0 fusion.22
  82.5 0.2 copy-done.10
  82.7 1.4 %multiply_reduce_fusion.1 = (f32[32,128]{1,0:T(8,128)S(1)}, f32[32,128]{1,0:T(8,128)S(1)}, f32[32,128]{1,0:T(8,128)S(1)}, f32[32,128]{1,0:T(8,128)S(1)}) fusion(s32[64,32,128]{2,1,0:T(8,128)S(1)} %copy-done.10, f32[64,32,128]{2,1,0:T(8,128)S(1)} %fusion.22), kind=kOutput, calls=%fused_computation.106 | output fusion | flops 27246592 | bytes 2162688 | tf_op jit(solution)/shard_map/jit(cumsum)/reduce_window_sum | solution.py:97
  84.1 25.4 %all-gather = f32[32,32,128]{2,1,0:T(8,128)S(1)} all-gather(f32[4,32,128]{2,1,0:T(8,128)S(1)} %pad_maximum_fusion.14), channel_id=2, replica_groups=mesh['view'=8,'wide'=32] {'view'}, dimensions={0}, use_global_device_ids=true | all-gather | bytes 589824 | tf_op jit(solution)/shard_map/all_gather | solution.py:111
  109.9 0.6 while.10
  110.5 0.6 pad_maximum_fusion.24
  (86 shorter events, 2.3 us)
Async XLA Ops:
  0.6 4.2 %copy-start.11 = (f32[64,32,128]{2,1,0:T(8,128)S(1)}, f32[64,32,128]{2,1,0:T(8,128)}, u32[]{:S(2)}) copy-start(f32[64,32,128]{2,1,0:T(8,128)} %param.9) | copy-start | bytes 3145732
  1.5 8.6 %collective-permute-start.5 = (f32[1,32,128]{2,1,0:T(8,128)S(1)}, f32[1,32,128]{2,1,0:T(8,128)S(1)}, u32[]{:S(2)}, u32[]{:S(2)}) collective-permute-start(f32[1,32,128]{2,1,0:T(8,128)S(1)} %get-tuple-element.84), channel_id=1, source_target_pairs={{32,0},{64,32},{96,64},{128,96},{160,128},{192,160},{224,192},{0,2... | collective-permute-start | bytes 49160 | tf_op jit(solution)/shard_map/ppermute | solution.py:18
  3.3 6.7 %collective-permute-start.4 = (f32[1,32,128]{2,1,0:T(8,128)S(1)}, f32[1,32,128]{2,1,0:T(8,128)S(1)}, u32[]{:S(2)}, u32[]{:S(2)}) collective-permute-start(f32[1,32,128]{2,1,0:T(8,128)S(1)} %get-tuple-element.85), channel_id=1, source_target_pairs={{0,32},{32,64},{64,96},{96,128},{128,160},{160,192},{192,224},{224... | collective-permute-start | bytes 49160 | tf_op jit(solution)/shard_map/ppermute | solution.py:16
  4.8 5.1 %copy-start.12 = (f32[64,32,128]{2,1,0:T(8,128)S(1)}, f32[64,32,128]{2,1,0:T(8,128)}, u32[]{:S(2)}) copy-start(f32[64,32,128]{2,1,0:T(8,128)} %param.6) | copy-start | bytes 3145732
  4.9 10.4 %copy-start = (f32[3,64,32,128]{3,2,1,0:T(8,128)S(1)}, f32[3,64,32,128]{3,2,1,0:T(8,128)}, u32[]{:S(2)}) copy-start(f32[3,64,32,128]{3,2,1,0:T(8,128)} %param.7) | copy-start | bytes 9437188
  5.9 9.4 %collective-permute-start = (f32[5,1,32,128]{3,2,1,0:T(8,128)S(1)}, f32[5,1,32,128]{3,2,1,0:T(8,128)S(1)}, u32[]{:S(2)}, u32[]{:S(2)}) collective-permute-start(f32[5,1,32,128]{3,2,1,0:T(8,128)S(1)} %get-tuple-element.44), channel_id=1, source_target_pairs={{0,32},{32,64},{64,96},{96,128},{128,160},{160,192},{192,224},{224... | collective-permute-start | bytes 245768 | tf_op jit(solution)/shard_map/ppermute | solution.py:16
  7.9 7.4 %collective-permute-start.1 = (f32[5,1,32,128]{3,2,1,0:T(8,128)S(1)}, f32[5,1,32,128]{3,2,1,0:T(8,128)S(1)}, u32[]{:S(2)}, u32[]{:S(2)}) collective-permute-start(f32[5,1,32,128]{3,2,1,0:T(8,128)S(1)} %get-tuple-element.45), channel_id=1, source_target_pairs={{32,0},{64,32},{96,64},{128,96},{160,128},{192,160},{224,192},{0,2... | collective-permute-start | bytes 245768 | tf_op jit(solution)/shard_map/ppermute | solution.py:18
  10.1 10.5 %collective-permute-start.6 = (f32[66,1,128]{2,1,0:T(1,128)S(1)}, f32[66,1,128]{2,1,0:T(1,128)S(1)}, u32[]{:S(2)}, u32[]{:S(2)}) collective-permute-start(f32[66,1,128]{2,1,0:T(1,128)S(1)} %get-tuple-element.76), channel_id=1, source_target_pairs={{0,1},{1,2},{2,3},{3,4},{4,5},{5,6},{6,7},{7,8},{8,9},{9,10},{10,1... | collective-permute-start | bytes 101384 | tf_op jit(solution)/shard_map/ppermute | solution.py:16
  10.2 10.5 %collective-permute-start.7 = (f32[66,1,128]{2,1,0:T(1,128)S(1)}, f32[66,1,128]{2,1,0:T(1,128)S(1)}, u32[]{:S(2)}, u32[]{:S(2)}) collective-permute-start(f32[66,1,128]{2,1,0:T(1,128)S(1)} %get-tuple-element.77), channel_id=1, source_target_pairs={{1,0},{2,1},{3,2},{4,3},{5,4},{6,5},{7,6},{8,7},{9,8},{10,9},{11,1... | collective-permute-start | bytes 101384 | tf_op jit(solution)/shard_map/ppermute | solution.py:18
  15.5 8.2 %collective-permute-start.2 = (f32[5,66,1,128]{3,2,1,0:T(1,128)S(1)}, f32[5,66,1,128]{3,2,1,0:T(1,128)S(1)}, u32[]{:S(2)}, u32[]{:S(2)}) collective-permute-start(f32[5,66,1,128]{3,2,1,0:T(1,128)S(1)} %get-tuple-element.42), channel_id=1, source_target_pairs={{0,1},{1,2},{2,3},{3,4},{4,5},{5,6},{6,7},{7,8},{8,9},{9,10},{10,1... | collective-permute-start | bytes 506888 | tf_op jit(solution)/shard_map/ppermute | solution.py:16
  15.6 8.1 %collective-permute-start.3 = (f32[5,66,1,128]{3,2,1,0:T(1,128)S(1)}, f32[5,66,1,128]{3,2,1,0:T(1,128)S(1)}, u32[]{:S(2)}, u32[]{:S(2)}) collective-permute-start(f32[5,66,1,128]{3,2,1,0:T(1,128)S(1)} %get-tuple-element.43), channel_id=1, source_target_pairs={{1,0},{2,1},{3,2},{4,3},{5,4},{6,5},{7,6},{8,7},{9,8},{10,9},{11,1... | collective-permute-start | bytes 506888 | tf_op jit(solution)/shard_map/ppermute | solution.py:18
  26.9 35.8 %copy-start.1 = (f32[66,34,128]{2,1,0:T(8,128)}, f32[66,34,128]{2,1,0:T(8,128)S(1)}, u32[]{:S(2)}) copy-start(f32[66,34,128]{2,1,0:T(8,128)S(1)} %get-tuple-element.38) | copy-start | bytes 3446788
  27.2 33.5 %copy-start.7 = (f32[1,65,34,128]{3,2,1,0:T(8,128)}, f32[1,65,34,128]{3,2,1,0:T(8,128)S(1)}, u32[]{:S(2)}) copy-start(f32[1,65,34,128]{3,2,1,0:T(8,128)S(1)} %get-tuple-element.31) | copy-start | bytes 3394564
  27.7 33.7 %copy-start.3 = (f32[66,33,128]{2,1,0:T(8,128)}, f32[66,33,128]{2,1,0:T(8,128)S(1)}, u32[]{:S(2)}) copy-start(f32[66,33,128]{2,1,0:T(8,128)S(1)} %get-tuple-element.33) | copy-start | bytes 3345412
  29.0 31.9 %copy-start.5 = (f32[66,34,127]{2,1,0:T(8,128)}, f32[66,34,127]{2,1,0:T(8,128)S(1)}, u32[]{:S(2)}) copy-start(f32[66,34,127]{2,1,0:T(8,128)S(1)} %get-tuple-element.35) | copy-start | bytes 3419860
  30.4 5.2 %collective-permute-start.8 = (f32[1,32,128]{2,1,0:T(8,128)S(1)}, f32[1,32,128]{2,1,0:T(8,128)S(1)}, u32[]{:S(2)}, u32[]{:S(2)}) collective-permute-start(f32[1,32,128]{2,1,0:T(8,128)S(1)} %get-tuple-element.82), channel_id=1, source_target_pairs={{0,32},{32,64},{64,96},{96,128},{128,160},{160,192},{192,224},{224... | collective-permute-start | bytes 49160 | tf_op jit(solution)/shard_map/ppermute | solution.py:16
  31.7 3.9 %collective-permute-start.9 = (f32[1,32,128]{2,1,0:T(8,128)S(1)}, f32[1,32,128]{2,1,0:T(8,128)S(1)}, u32[]{:S(2)}, u32[]{:S(2)}) collective-permute-start(f32[1,32,128]{2,1,0:T(8,128)S(1)} %get-tuple-element.83), channel_id=1, source_target_pairs={{32,0},{64,32},{96,64},{128,96},{160,128},{192,160},{224,192},{0,2... | collective-permute-start | bytes 49160 | tf_op jit(solution)/shard_map/ppermute | solution.py:18
  35.7 6.7 %collective-permute-start.10 = (f32[66,1,128]{2,1,0:T(1,128)S(1)}, f32[66,1,128]{2,1,0:T(1,128)S(1)}, u32[]{:S(2)}, u32[]{:S(2)}) collective-permute-start(f32[66,1,128]{2,1,0:T(1,128)S(1)} %get-tuple-element.74), channel_id=1, source_target_pairs={{0,1},{1,2},{2,3},{3,4},{4,5},{5,6},{6,7},{7,8},{8,9},{9,10},{10,1... | collective-permute-start | bytes 101384 | tf_op jit(solution)/shard_map/ppermute | solution.py:16
  35.7 6.7 %collective-permute-start.11 = (f32[66,1,128]{2,1,0:T(1,128)S(1)}, f32[66,1,128]{2,1,0:T(1,128)S(1)}, u32[]{:S(2)}, u32[]{:S(2)}) collective-permute-start(f32[66,1,128]{2,1,0:T(1,128)S(1)} %get-tuple-element.75), channel_id=1, source_target_pairs={{1,0},{2,1},{3,2},{4,3},{5,4},{6,5},{7,6},{8,7},{9,8},{10,9},{11,1... | collective-permute-start | bytes 101384 | tf_op jit(solution)/shard_map/ppermute | solution.py:18
  45.7 5.0 %collective-permute-start.12 = (f32[1,32,128]{2,1,0:T(8,128)S(1)}, f32[1,32,128]{2,1,0:T(8,128)S(1)}, u32[]{:S(2)}, u32[]{:S(2)}) collective-permute-start(f32[1,32,128]{2,1,0:T(8,128)S(1)} %get-tuple-element.80), channel_id=1, source_target_pairs={{0,32},{32,64},{64,96},{96,128},{128,160},{160,192},{192,224},{224... | collective-permute-start | bytes 49160 | tf_op jit(solution)/shard_map/ppermute | solution.py:16
  48.7 4.9 %collective-permute-start.13 = (f32[1,32,128]{2,1,0:T(8,128)S(1)}, f32[1,32,128]{2,1,0:T(8,128)S(1)}, u32[]{:S(2)}, u32[]{:S(2)}) collective-permute-start(f32[1,32,128]{2,1,0:T(8,128)S(1)} %get-tuple-element.81), channel_id=1, source_target_pairs={{32,0},{64,32},{96,64},{128,96},{160,128},{192,160},{224,192},{0,2... | collective-permute-start | bytes 49160 | tf_op jit(solution)/shard_map/ppermute | solution.py:18
  53.7 6.7 %collective-permute-start.14 = (f32[66,1,128]{2,1,0:T(1,128)S(1)}, f32[66,1,128]{2,1,0:T(1,128)S(1)}, u32[]{:S(2)}, u32[]{:S(2)}) collective-permute-start(f32[66,1,128]{2,1,0:T(1,128)S(1)} %get-tuple-element.72), channel_id=1, source_target_pairs={{0,1},{1,2},{2,3},{3,4},{4,5},{5,6},{6,7},{7,8},{8,9},{9,10},{10,1... | collective-permute-start | bytes 101384 | tf_op jit(solution)/shard_map/ppermute | solution.py:16
  53.8 6.7 %collective-permute-start.15 = (f32[66,1,128]{2,1,0:T(1,128)S(1)}, f32[66,1,128]{2,1,0:T(1,128)S(1)}, u32[]{:S(2)}, u32[]{:S(2)}) collective-permute-start(f32[66,1,128]{2,1,0:T(1,128)S(1)} %get-tuple-element.73), channel_id=1, source_target_pairs={{1,0},{2,1},{3,2},{4,3},{5,4},{6,5},{7,6},{8,7},{9,8},{10,9},{11,1... | collective-permute-start | bytes 101384 | tf_op jit(solution)/shard_map/ppermute | solution.py:18
  63.9 3.8 %collective-permute-start.16 = (f32[1,32,128]{2,1,0:T(8,128)S(1)}, f32[1,32,128]{2,1,0:T(8,128)S(1)}, u32[]{:S(2)}, u32[]{:S(2)}) collective-permute-start(f32[1,32,128]{2,1,0:T(8,128)S(1)} %get-tuple-element.78), channel_id=1, source_target_pairs={{0,32},{32,64},{64,96},{96,128},{128,160},{160,192},{192,224},{224... | collective-permute-start | bytes 49160 | tf_op jit(solution)/shard_map/ppermute | solution.py:16
  66.0 3.7 %collective-permute-start.17 = (f32[1,32,128]{2,1,0:T(8,128)S(1)}, f32[1,32,128]{2,1,0:T(8,128)S(1)}, u32[]{:S(2)}, u32[]{:S(2)}) collective-permute-start(f32[1,32,128]{2,1,0:T(8,128)S(1)} %get-tuple-element.79), channel_id=1, source_target_pairs={{32,0},{64,32},{96,64},{128,96},{160,128},{192,160},{224,192},{0,2... | collective-permute-start | bytes 49160 | tf_op jit(solution)/shard_map/ppermute | solution.py:18
  69.7 6.7 %collective-permute-start.18 = (f32[66,1,128]{2,1,0:T(1,128)S(1)}, f32[66,1,128]{2,1,0:T(1,128)S(1)}, u32[]{:S(2)}, u32[]{:S(2)}) collective-permute-start(f32[66,1,128]{2,1,0:T(1,128)S(1)} %get-tuple-element.70), channel_id=1, source_target_pairs={{0,1},{1,2},{2,3},{3,4},{4,5},{5,6},{6,7},{7,8},{8,9},{9,10},{10,1... | collective-permute-start | bytes 101384 | tf_op jit(solution)/shard_map/ppermute | solution.py:16
  69.8 6.7 %collective-permute-start.19 = (f32[66,1,128]{2,1,0:T(1,128)S(1)}, f32[66,1,128]{2,1,0:T(1,128)S(1)}, u32[]{:S(2)}, u32[]{:S(2)}) collective-permute-start(f32[66,1,128]{2,1,0:T(1,128)S(1)} %get-tuple-element.71), channel_id=1, source_target_pairs={{1,0},{2,1},{3,2},{4,3},{5,4},{6,5},{7,6},{8,7},{9,8},{10,9},{11,1... | collective-permute-start | bytes 101384 | tf_op jit(solution)/shard_map/ppermute | solution.py:18
  74.9 1.8 %copy-start.8 = (f32[1,65,34,128]{3,2,1,0:T(8,128)S(1)}, f32[1,65,34,128]{3,2,1,0:T(8,128)}, u32[]{:S(2)}) copy-start(f32[1,65,34,128]{3,2,1,0:T(8,128)} %copy-done.7) | copy-start | bytes 3394564
  76.7 1.3 %copy-start.6 = (f32[66,34,127]{2,1,0:T(8,128)S(1)}, f32[66,34,127]{2,1,0:T(8,128)}, u32[]{:S(2)}) copy-start(f32[66,34,127]{2,1,0:T(8,128)} %copy-done.5) | copy-start | bytes 3419860
  78.1 1.3 %copy-start.4 = (f32[66,33,128]{2,1,0:T(8,128)S(1)}, f32[66,33,128]{2,1,0:T(8,128)}, u32[]{:S(2)}) copy-start(f32[66,33,128]{2,1,0:T(8,128)} %copy-done.3) | copy-start | bytes 3345412
  80.2 1.3 %copy-start.2 = (f32[66,34,128]{2,1,0:T(8,128)S(1)}, f32[66,34,128]{2,1,0:T(8,128)}, u32[]{:S(2)}) copy-start(f32[66,34,128]{2,1,0:T(8,128)} %copy-done.1) | copy-start | bytes 3446788
  81.5 1.2 %copy-start.10 = (s32[64,32,128]{2,1,0:T(8,128)S(1)}, s32[64,32,128]{2,1,0:T(8,128)}, u32[]{:S(2)}) copy-start(s32[64,32,128]{2,1,0:T(8,128)} %param.8) | copy-start | bytes 3145732
  82.7 1.4 %copy-start.9 = (f32[64,32,128]{2,1,0:T(8,128)}, f32[64,32,128]{2,1,0:T(8,128)S(1)}, u32[]{:S(2)}) copy-start(f32[64,32,128]{2,1,0:T(8,128)S(1)} %fusion.22) | copy-start | bytes 3145732
  84.1 25.8 %copy-start.13 = (f32[4,32,16]{1,2,0:T(8,128)S(1)}, f32[4,32,16]{1,2,0:T(8,128)}, u32[]{:S(2)}) copy-start(f32[4,32,16]{1,2,0:T(8,128)} %constant.9.clone.1) | copy-start | bytes 24580
where the time goes:
time: 111 us
  starting transfers between devices  40.9 us (37%)
  blocking collectives  25.4 us (23%)
  other arithmetic  17.7 us (16%)
  waiting for transfers between devices  17.6 us (16%)
  local copies, waits for them, and re-layouts  8.11 us (7%)
  between operations  1.16 us (1%)
    ppermute x10, starting transfers between devices, padded_2(): lax.ppermute(head, axis, [((i + 1) % count, i) for i in range(count)])  31.9 us
    all_gather x1, blocking collectives, on_device(): pieces = lax.all_gather(partial_value[None], 'view', axis=0, tiled=True)  25.4 us
    ppermute x10, waiting for transfers between devices, padded_2(): lax.ppermute(tail, axis, [(i, (i + 1) % count) for i in range(count)])  12.6 us
    ppermute x10, starting transfers between devices, padded_2(): lax.ppermute(tail, axis, [(i, (i + 1) % count) for i in range(count)])  8.96 us
    ppermute x10, waiting for transfers between devices, padded_2(): lax.ppermute(head, axis, [((i + 1) % count, i) for i in range(count)])  4.99 us
    mul x4, other arithmetic, advance(): open_cells[1:-1, 1:-1]  4.2 us
    concatenate x5, other arithmetic, padded_2(): jnp.concatenate([lax.ppermute(tail, axis, [(i, (i + 1) % count) for i in...  3.6 us
    unnamed x31, local copies, waits for them, and re-layouts  3.31 us
  transfers between devices with their start and end apart: 20, of which 9 were waited for; matrix products, arithmetic and copies ran while one was open for 3% of the time, Pallas kernels for 0%

commit v1 on v0

--- a/solution.py
+++ b/solution.py
@@ -108,7 +108,11 @@
     height = partial_value.shape[2]
     block_width = height // view_count
     position = lax.axis_index("view")
-    pieces = lax.all_gather(partial_value[None], "view", axis=0, tiled=True)
+    part = partial_value[None]
+    size = lax.axis_size("view")
+    blocks = jnp.stack([part for _ in range(size)])
+    blocks = lax.all_to_all(blocks, "view", split_axis=0, concat_axis=0)
+    pieces = jnp.concatenate(blocks, axis=0)
     mine = lax.dynamic_slice_in_dim(pieces, position * block_width, block_width, 3)
     picture = finish_pixels(fold_in_order(mine))
     return (current, picture)

time: 111 us -> 103 us (0.928)
  the two profiles are of different devices: /device:TPU:32 before, /device:TPU:31 now
where the time goes in v1:
time: 103 us; the launch traced here: 102 us
  waiting for transfers between devices  44.1 us (43%)
  starting transfers between devices  32.6 us (32%)
  other arithmetic  18.1 us (18%)
  local copies, waits for them, and re-layouts  6.04 us (6%)
  between operations  1.05 us (1%)
    ppermute x10, waiting for transfers between devices, padded_2(): lax.ppermute(head, axis, [((i + 1) % count, i) for i in range(count)])  24.1 us
    ppermute x10, starting transfers between devices, padded_2(): lax.ppermute(head, axis, [((i + 1) % count, i) for i in range(count)])  16.3 us
    all_to_all x1, waiting for transfers between devices, on_device(): blocks = lax.all_to_all(blocks, 'view', split_axis=0, concat_axis=0)  13 us
    ppermute x10, starting transfers between devices, padded_2(): lax.ppermute(tail, axis, [(i, (i + 1) % count) for i in range(count)])  11.5 us
    ppermute x10, waiting for transfers between devices, padded_2(): lax.ppermute(tail, axis, [(i, (i + 1) % count) for i in range(count)])  6.91 us
    all_to_all x1, starting transfers between devices, on_device(): blocks = lax.all_to_all(blocks, 'view', split_axis=0, concat_axis=0)  4.84 us
    mul x4, other arithmetic, advance(): open_cells[1:-1, 1:-1]  4.54 us
    concatenate x5, other arithmetic, padded_2(): jnp.concatenate([lax.ppermute(tail, axis, [(i, (i + 1) % count) for i in...  3.58 us
  transfers between devices with their start and end apart: 21, of which 14 were waited for; matrix products, arithmetic and copies ran while one was open for 3% of the time, Pallas kernels for 0%

profile of v1, /device:TPU:31, one launch (start us, length us, event | category | flops | bytes accessed | tf_op | source)
XLA Modules:
  0.0 102.2 jit_solution(6594224050040940230)
XLA Ops:
  0.6 0.8 fusion.57
  1.5 5.6 %collective-permute-start.5 = (f32[1,32,128]{2,1,0:T(8,128)S(1)}, f32[1,32,128]{2,1,0:T(8,128)S(1)}, u32[]{:S(2)}, u32[]{:S(2)}) collective-permute-start(f32[1,32,128]{2,1,0:T(8,128)S(1)} %get-tuple-element.84), channel_id=1, source_target_pairs={{32,0},{64,32},{96,64},{128,96},{160,128},{192,160},{224,192},{0,2... | collective-permute-start | bytes 49160 | tf_op jit(solution)/shard_map/ppermute | solution.py:18
  7.0 1.3 %convert_bitcast_fusion = f32[1,64,32,128]{3,2,1,0:T(8,128)S(1)} fusion(s32[64,32,128]{2,1,0:T(8,128)} %param.8), kind=kLoop, calls=%fused_computation.110 | loop fusion | flops 524288 | bytes 2097152 | tf_op jit(solution)/shard_map/broadcast_in_dim | solution.py:91
  8.4 1.0 pad_maximum_fusion.13
  9.5 2.7 %collective-permute-start.1 = (f32[5,1,32,128]{3,2,1,0:T(8,128)S(1)}, f32[5,1,32,128]{3,2,1,0:T(8,128)S(1)}, u32[]{:S(2)}, u32[]{:S(2)}) collective-permute-start(f32[5,1,32,128]{3,2,1,0:T(8,128)S(1)} %get-tuple-element.45), channel_id=1, source_target_pairs={{32,0},{64,32},{96,64},{128,96},{160,128},{192,160},{224,192},{0,2... | collective-permute-start | bytes 245768 | tf_op jit(solution)/shard_map/ppermute | solution.py:18
  12.4 1.3 %collective-permute-start.6 = (f32[66,1,128]{2,1,0:T(1,128)S(1)}, f32[66,1,128]{2,1,0:T(1,128)S(1)}, u32[]{:S(2)}, u32[]{:S(2)}) collective-permute-start(f32[66,1,128]{2,1,0:T(1,128)S(1)} %get-tuple-element.76), channel_id=1, source_target_pairs={{0,1},{1,2},{2,3},{3,4},{4,5},{5,6},{6,7},{7,8},{8,9},{9,10},{10,1... | collective-permute-start | bytes 101384 | tf_op jit(solution)/shard_map/ppermute | solution.py:16
  13.8 0.3 collective-permute-start.7
  14.1 0.2 pad_maximum_fusion.10
  14.4 4.8 %collective-permute-start.2 = (f32[5,66,1,128]{3,2,1,0:T(1,128)S(1)}, f32[5,66,1,128]{3,2,1,0:T(1,128)S(1)}, u32[]{:S(2)}, u32[]{:S(2)}) collective-permute-start(f32[5,66,1,128]{3,2,1,0:T(1,128)S(1)} %get-tuple-element.42), channel_id=1, source_target_pairs={{0,1},{1,2},{2,3},{3,4},{4,5},{5,6},{6,7},{7,8},{8,9},{9,10},{10,1... | collective-permute-start | bytes 506888 | tf_op jit(solution)/shard_map/ppermute | solution.py:16
  19.2 1.3 %collective-permute-done.7 = f32[66,1,128]{2,1,0:T(1,128)S(1)} collective-permute-done((f32[66,1,128]{2,1,0:T(1,128)S(1)}, f32[66,1,128]{2,1,0:T(1,128)S(1)}, u32[]{:S(2)}, u32[]{:S(2)}) %collective-permute-start.7) | collective-permute-done | bytes 33824 | tf_op jit(solution)/shard_map/ppermute | solution.py:18
  20.7 0.8 collective-permute-done.2
  21.5 5.8 %collective-permute-done.3 = f32[5,66,1,128]{3,2,1,0:T(1,128)S(1)} collective-permute-done((f32[5,66,1,128]{3,2,1,0:T(1,128)S(1)}, f32[5,66,1,128]{3,2,1,0:T(1,128)S(1)}, u32[]{:S(2)}, u32[]{:S(2)}) %collective-permute-start.3) | collective-permute-done | bytes 168992 | tf_op jit(solution)/shard_map/ppermute | solution.py:18
  27.3 2.7 %pad_maximum_fusion.1 = f32[5,66,34,128]{3,2,1,0:T(8,128)S(1)} fusion(f32[5,66,1,128]{3,2,1,0:T(1,128)S(1)} %collective-permute-done.3, f32[5,1,32,128]{3,2,1,0:T(8,128)S(1)} %collective-permute-done.1, f32[1,64,32,128]{3,2,1,0:T(8,128)S(1)} %bitcast.45, f32[1,64,32,128]{3,2,1,0:T(8,128)S(1)} %convert_bitcast_fusion, f32[3,64,32,128]{3,2,1,0:T(8,128)S(1)} %copy-done, ...), kind=kLoop, calls=%fused_computation.7 | loop fusion | flops 8616960 | bytes 11489280 | tf_op jit(solution)/shard_map/concatenate | solution.py:14
  30.0 0.4 slice_bitcast_fusion.1
  30.4 0.3 fusion.14
  30.7 0.6 fusion.7
  31.3 0.2 fusion.48
  31.8 0.8 fusion.6
  32.6 0.4 pad_slice_fusion.7
  33.0 1.2 %fusion.37 = f32[64,32,128]{2,1,0:T(8,128)S(1)} fusion(f32[66,34,128]{2,1,0:T(8,128)S(1)} %get-tuple-element.61, f32[66,34,128]{2,1,0:T(8,128)S(1)} %get-tuple-element.60, f32[66,32,128]{2,1,0:T(8,128)S(1)} %get-tuple-element.59, f32[66,32,128]{2,1,0:T(8,128)S(1)} %get-tuple-element.58, f32[64,32,128]{2,1,0:T(8,128)S(1)} %copy-done.4, ...), kind=kLoop, calls=%fused_computation.100 | loop fusion | flops 2097152 | bytes 10485760 | tf_op jit(solution)/shard_map/mul | solution.py:42
  34.2 0.3 collective-permute-start.8
  34.5 2.7 %collective-permute-start.9 = (f32[1,32,128]{2,1,0:T(8,128)S(1)}, f32[1,32,128]{2,1,0:T(8,128)S(1)}, u32[]{:S(2)}, u32[]{:S(2)}) collective-permute-start(f32[1,32,128]{2,1,0:T(8,128)S(1)} %get-tuple-element.83), channel_id=1, source_target_pairs={{32,0},{64,32},{96,64},{128,96},{160,128},{192,160},{224,192},{0,2... | collective-permute-start | bytes 49160 | tf_op jit(solution)/shard_map/ppermute | solution.py:18
  37.2 1.1 %collective-permute-done.8 = f32[1,32,128]{2,1,0:T(8,128)S(1)} collective-permute-done((f32[1,32,128]{2,1,0:T(8,128)S(1)}, f32[1,32,128]{2,1,0:T(8,128)S(1)}, u32[]{:S(2)}, u32[]{:S(2)}) %collective-permute-start.8) | collective-permute-done | bytes 16416 | tf_op jit(solution)/shard_map/ppermute | solution.py:16
  38.3 1.2 %collective-permute-start.10 = (f32[66,1,128]{2,1,0:T(1,128)S(1)}, f32[66,1,128]{2,1,0:T(1,128)S(1)}, u32[]{:S(2)}, u32[]{:S(2)}) collective-permute-start(f32[66,1,128]{2,1,0:T(1,128)S(1)} %get-tuple-element.74), channel_id=1, source_target_pairs={{0,1},{1,2},{2,3},{3,4},{4,5},{5,6},{6,7},{7,8},{8,9},{9,10},{10,1... | collective-permute-start | bytes 101384 | tf_op jit(solution)/shard_map/ppermute | solution.py:16
  39.6 1.0 %collective-permute-done.10 = f32[66,1,128]{2,1,0:T(1,128)S(1)} collective-permute-done((f32[66,1,128]{2,1,0:T(1,128)S(1)}, f32[66,1,128]{2,1,0:T(1,128)S(1)}, u32[]{:S(2)}, u32[]{:S(2)}) %collective-permute-start.10) | collective-permute-done | bytes 33824 | tf_op jit(solution)/shard_map/ppermute | solution.py:16
  40.6 5.6 %collective-permute-done.11 = f32[66,1,128]{2,1,0:T(1,128)S(1)} collective-permute-done((f32[66,1,128]{2,1,0:T(1,128)S(1)}, f32[66,1,128]{2,1,0:T(1,128)S(1)}, u32[]{:S(2)}, u32[]{:S(2)}) %collective-permute-start.11) | collective-permute-done | bytes 33824 | tf_op jit(solution)/shard_map/ppermute | solution.py:18
  46.2 0.3 fusion.8
  46.6 0.2 fusion.47
  46.8 0.2 pad_maximum_fusion.3
  47.0 0.3 fusion.13
  47.3 0.4 fusion.5
  48.0 0.4 pad_slice_fusion.5
  48.4 1.1 %fusion.32 = f32[64,32,128]{2,1,0:T(8,128)S(1)} fusion(f32[66,34,128]{2,1,0:T(8,128)S(1)} %get-tuple-element.57, f32[66,34,128]{2,1,0:T(8,128)S(1)} %get-tuple-element.56, f32[66,32,128]{2,1,0:T(8,128)S(1)} %get-tuple-element.55, f32[66,32,128]{2,1,0:T(8,128)S(1)} %get-tuple-element.54, f32[64,32,128]{2,1,0:T(8,128)S(1)} %fusion.37, ...), kind=kLoop, calls=%fused_computation.92 | loop fusion | flops 2097152 | bytes 10485760 | tf_op jit(solution)/shard_map/mul | solution.py:42
  49.7 3.0 %collective-permute-start.13 = (f32[1,32,128]{2,1,0:T(8,128)S(1)}, f32[1,32,128]{2,1,0:T(8,128)S(1)}, u32[]{:S(2)}, u32[]{:S(2)}) collective-permute-start(f32[1,32,128]{2,1,0:T(8,128)S(1)} %get-tuple-element.81), channel_id=1, source_target_pairs={{32,0},{64,32},{96,64},{128,96},{160,128},{192,160},{224,192},{0,2... | collective-permute-start | bytes 49160 | tf_op jit(solution)/shard_map/ppermute | solution.py:18
  52.7 1.0 %collective-permute-done.12 = f32[1,32,128]{2,1,0:T(8,128)S(1)} collective-permute-done((f32[1,32,128]{2,1,0:T(8,128)S(1)}, f32[1,32,128]{2,1,0:T(8,128)S(1)}, u32[]{:S(2)}, u32[]{:S(2)}) %collective-permute-start.12) | collective-permute-done | bytes 16416 | tf_op jit(solution)/shard_map/ppermute | solution.py:16
  53.8 1.0 collective-permute-start.14
  54.7 1.0 %collective-permute-done.14 = f32[66,1,128]{2,1,0:T(1,128)S(1)} collective-permute-done((f32[66,1,128]{2,1,0:T(1,128)S(1)}, f32[66,1,128]{2,1,0:T(1,128)S(1)}, u32[]{:S(2)}, u32[]{:S(2)}) %collective-permute-start.14) | collective-permute-done | bytes 33824 | tf_op jit(solution)/shard_map/ppermute | solution.py:16
  55.8 5.6 %collective-permute-done.15 = f32[66,1,128]{2,1,0:T(1,128)S(1)} collective-permute-done((f32[66,1,128]{2,1,0:T(1,128)S(1)}, f32[66,1,128]{2,1,0:T(1,128)S(1)}, u32[]{:S(2)}, u32[]{:S(2)}) %collective-permute-start.15) | collective-permute-done | bytes 33824 | tf_op jit(solution)/shard_map/ppermute | solution.py:18
  61.4 0.2 pad_maximum_fusion.4
  61.6 0.3 fusion.12
  61.9 0.4 fusion.4
  62.4 0.4 fusion.9
  62.7 0.2 fusion.46
  63.1 0.4 pad_slice_fusion.3
  63.6 1.1 %fusion.27 = f32[64,32,128]{2,1,0:T(8,128)S(1)} fusion(f32[66,34,128]{2,1,0:T(8,128)S(1)} %get-tuple-element.53, f32[66,34,128]{2,1,0:T(8,128)S(1)} %get-tuple-element.52, f32[66,32,128]{2,1,0:T(8,128)S(1)} %get-tuple-element.51, f32[66,32,128]{2,1,0:T(8,128)S(1)} %get-tuple-element.50, f32[64,32,128]{2,1,0:T(8,128)S(1)} %fusion.32, ...), kind=kLoop, calls=%fused_computation.84 | loop fusion | flops 2097152 | bytes 10485760 | tf_op jit(solution)/shard_map/mul | solution.py:42
  64.7 1.5 %collective-permute-start.16 = (f32[1,32,128]{2,1,0:T(8,128)S(1)}, f32[1,32,128]{2,1,0:T(8,128)S(1)}, u32[]{:S(2)}, u32[]{:S(2)}) collective-permute-start(f32[1,32,128]{2,1,0:T(8,128)S(1)} %get-tuple-element.78), channel_id=1, source_target_pairs={{0,32},{32,64},{64,96},{96,128},{128,160},{160,192},{192,224},{224... | collective-permute-start | bytes 49160 | tf_op jit(solution)/shard_map/ppermute | solution.py:16
  66.3 1.9 %collective-permute-start.17 = (f32[1,32,128]{2,1,0:T(8,128)S(1)}, f32[1,32,128]{2,1,0:T(8,128)S(1)}, u32[]{:S(2)}, u32[]{:S(2)}) collective-permute-start(f32[1,32,128]{2,1,0:T(8,128)S(1)} %get-tuple-element.79), channel_id=1, source_target_pairs={{32,0},{64,32},{96,64},{128,96},{160,128},{192,160},{224,192},{0,2... | collective-permute-start | bytes 49160 | tf_op jit(solution)/shard_map/ppermute | solution.py:18
  68.2 0.8 collective-permute-done.16
  69.2 1.2 %collective-permute-start.18 = (f32[66,1,128]{2,1,0:T(1,128)S(1)}, f32[66,1,128]{2,1,0:T(1,128)S(1)}, u32[]{:S(2)}, u32[]{:S(2)}) collective-permute-start(f32[66,1,128]{2,1,0:T(1,128)S(1)} %get-tuple-element.70), channel_id=1, source_target_pairs={{0,1},{1,2},{2,3},{3,4},{4,5},{5,6},{6,7},{7,8},{8,9},{9,10},{10,1... | collective-permute-start | bytes 101384 | tf_op jit(solution)/shard_map/ppermute | solution.py:16
  70.4 1.0 %collective-permute-done.18 = f32[66,1,128]{2,1,0:T(1,128)S(1)} collective-permute-done((f32[66,1,128]{2,1,0:T(1,128)S(1)}, f32[66,1,128]{2,1,0:T(1,128)S(1)}, u32[]{:S(2)}, u32[]{:S(2)}) %collective-permute-start.18) | collective-permute-done | bytes 33824 | tf_op jit(solution)/shard_map/ppermute | solution.py:16
  71.4 5.6 %collective-permute-done.19 = f32[66,1,128]{2,1,0:T(1,128)S(1)} collective-permute-done((f32[66,1,128]{2,1,0:T(1,128)S(1)}, f32[66,1,128]{2,1,0:T(1,128)S(1)}, u32[]{:S(2)}, u32[]{:S(2)}) %collective-permute-start.19) | collective-permute-done | bytes 33824 | tf_op jit(solution)/shard_map/ppermute | solution.py:18
  77.1 0.2 pad_maximum_fusion.5
  77.3 0.3 fusion.11
  77.6 0.4 fusion.3
  78.0 0.4 fusion.10
  78.4 0.2 fusion.45
  78.8 0.4 pad_slice_fusion.1
  79.3 1.1 %fusion.22 = f32[64,32,128]{2,1,0:T(8,128)S(1)} fusion(f32[66,34,128]{2,1,0:T(8,128)S(1)} %get-tuple-element.49, f32[66,34,128]{2,1,0:T(8,128)S(1)} %get-tuple-element.48, f32[66,32,128]{2,1,0:T(8,128)S(1)} %get-tuple-element.47, f32[66,32,128]{2,1,0:T(8,128)S(1)} %get-tuple-element.46, f32[64,32,128]{2,1,0:T(8,128)S(1)} %fusion.27, ...), kind=kLoop, calls=%fused_computation.76 | loop fusion | flops 2097152 | bytes 10485760 | tf_op jit(solution)/shard_map/mul | solution.py:42
  80.5 1.4 %multiply_reduce_fusion.1 = (f32[32,128]{1,0:T(8,128)S(1)}, f32[32,128]{1,0:T(8,128)S(1)}, f32[32,128]{1,0:T(8,128)S(1)}, f32[32,128]{1,0:T(8,128)S(1)}) fusion(s32[64,32,128]{2,1,0:T(8,128)S(1)} %copy-done.2, f32[64,32,128]{2,1,0:T(8,128)S(1)} %fusion.22), kind=kOutput, calls=%fused_computation.106 | output fusion | flops 27246592 | bytes 2162688 | tf_op jit(solution)/shard_map/jit(cumsum)/reduce_window_sum | solution.py:97
  81.9 0.8 stack.20
  82.7 4.8 %all-to-all-start = ((f32[8,1,4,32,128]{4,3,2,1,0:T(8,128)}), f32[8,1,4,32,128]{4,3,2,1,0:T(8,128)S(1)}, u32[]{:S(2)}, u32[]{:S(2)}) async-start(f32[8,1,4,32,128]{4,3,2,1,0:T(8,128)} %stack.20), calls=%async_computation | async-start | bytes 1048576 | tf_op jit(solution)/shard_map/all_to_all | solution.py:114
  87.6 13.0 %all-to-all-done = f32[8,1,4,32,128]{4,3,2,1,0:T(8,128)S(1)} async-done(((f32[8,1,4,32,128]{4,3,2,1,0:T(8,128)}), f32[8,1,4,32,128]{4,3,2,1,0:T(8,128)S(1)}, u32[]{:S(2)}, u32[]{:S(2)}) %all-to-all-start) | async-done | bytes 524320 | tf_op jit(solution)/shard_map/all_to_all | solution.py:114
  101.0 0.6 while.10
  101.6 0.6 pad_maximum_fusion.24
  (72 shorter events, 2.3 us)
Async XLA Ops:
  0.6 7.8 %copy-start.3 = (f32[64,32,128]{2,1,0:T(8,128)S(1)}, f32[64,32,128]{2,1,0:T(8,128)}, u32[]{:S(2)}) copy-start(f32[64,32,128]{2,1,0:T(8,128)} %param.9) | copy-start | bytes 3145732
  1.5 10.9 %collective-permute-start.5 = (f32[1,32,128]{2,1,0:T(8,128)S(1)}, f32[1,32,128]{2,1,0:T(8,128)S(1)}, u32[]{:S(2)}, u32[]{:S(2)}) collective-permute-start(f32[1,32,128]{2,1,0:T(8,128)S(1)} %get-tuple-element.84), channel_id=1, source_target_pairs={{32,0},{64,32},{96,64},{128,96},{160,128},{192,160},{224,192},{0,2... | collective-permute-start | bytes 49160 | tf_op jit(solution)/shard_map/ppermute | solution.py:18
  7.0 5.2 %collective-permute-start.4 = (f32[1,32,128]{2,1,0:T(8,128)S(1)}, f32[1,32,128]{2,1,0:T(8,128)S(1)}, u32[]{:S(2)}, u32[]{:S(2)}) collective-permute-start(f32[1,32,128]{2,1,0:T(8,128)S(1)} %get-tuple-element.85), channel_id=1, source_target_pairs={{0,32},{32,64},{64,96},{96,128},{128,160},{160,192},{192,224},{224... | collective-permute-start | bytes 49160 | tf_op jit(solution)/shard_map/ppermute | solution.py:16
  8.4 3.9 %copy-start.4 = (f32[64,32,128]{2,1,0:T(8,128)S(1)}, f32[64,32,128]{2,1,0:T(8,128)}, u32[]{:S(2)}) copy-start(f32[64,32,128]{2,1,0:T(8,128)} %param.6) | copy-start | bytes 3145732
  8.4 5.7 %copy-start = (f32[3,64,32,128]{3,2,1,0:T(8,128)S(1)}, f32[3,64,32,128]{3,2,1,0:T(8,128)}, u32[]{:S(2)}) copy-start(f32[3,64,32,128]{3,2,1,0:T(8,128)} %param.7) | copy-start | bytes 9437188
  9.4 4.7 %collective-permute-start = (f32[5,1,32,128]{3,2,1,0:T(8,128)S(1)}, f32[5,1,32,128]{3,2,1,0:T(8,128)S(1)}, u32[]{:S(2)}, u32[]{:S(2)}) collective-permute-start(f32[5,1,32,128]{3,2,1,0:T(8,128)S(1)} %get-tuple-element.44), channel_id=1, source_target_pairs={{0,32},{32,64},{64,96},{96,128},{128,160},{160,192},{192,224},{224... | collective-permute-start | bytes 245768 | tf_op jit(solution)/shard_map/ppermute | solution.py:16
  9.5 4.6 %collective-permute-start.1 = (f32[5,1,32,128]{3,2,1,0:T(8,128)S(1)}, f32[5,1,32,128]{3,2,1,0:T(8,128)S(1)}, u32[]{:S(2)}, u32[]{:S(2)}) collective-permute-start(f32[5,1,32,128]{3,2,1,0:T(8,128)S(1)} %get-tuple-element.45), channel_id=1, source_target_pairs={{32,0},{64,32},{96,64},{128,96},{160,128},{192,160},{224,192},{0,2... | collective-permute-start | bytes 245768 | tf_op jit(solution)/shard_map/ppermute | solution.py:18
  12.4 6.7 %collective-permute-start.6 = (f32[66,1,128]{2,1,0:T(1,128)S(1)}, f32[66,1,128]{2,1,0:T(1,128)S(1)}, u32[]{:S(2)}, u32[]{:S(2)}) collective-permute-start(f32[66,1,128]{2,1,0:T(1,128)S(1)} %get-tuple-element.76), channel_id=1, source_target_pairs={{0,1},{1,2},{2,3},{3,4},{4,5},{5,6},{6,7},{7,8},{8,9},{9,10},{10,1... | collective-permute-start | bytes 101384 | tf_op jit(solution)/shard_map/ppermute | solution.py:16
  13.8 6.7 %collective-permute-start.7 = (f32[66,1,128]{2,1,0:T(1,128)S(1)}, f32[66,1,128]{2,1,0:T(1,128)S(1)}, u32[]{:S(2)}, u32[]{:S(2)}) collective-permute-start(f32[66,1,128]{2,1,0:T(1,128)S(1)} %get-tuple-element.77), channel_id=1, source_target_pairs={{1,0},{2,1},{3,2},{4,3},{5,4},{6,5},{7,6},{8,7},{9,8},{10,9},{11,1... | collective-permute-start | bytes 101384 | tf_op jit(solution)/shard_map/ppermute | solution.py:18
  14.4 7.1 %collective-permute-start.2 = (f32[5,66,1,128]{3,2,1,0:T(1,128)S(1)}, f32[5,66,1,128]{3,2,1,0:T(1,128)S(1)}, u32[]{:S(2)}, u32[]{:S(2)}) collective-permute-start(f32[5,66,1,128]{3,2,1,0:T(1,128)S(1)} %get-tuple-element.42), channel_id=1, source_target_pairs={{0,1},{1,2},{2,3},{3,4},{4,5},{5,6},{6,7},{7,8},{8,9},{9,10},{10,1... | collective-permute-start | bytes 506888 | tf_op jit(solution)/shard_map/ppermute | solution.py:16
  19.2 8.1 %collective-permute-start.3 = (f32[5,66,1,128]{3,2,1,0:T(1,128)S(1)}, f32[5,66,1,128]{3,2,1,0:T(1,128)S(1)}, u32[]{:S(2)}, u32[]{:S(2)}) collective-permute-start(f32[5,66,1,128]{3,2,1,0:T(1,128)S(1)} %get-tuple-element.43), channel_id=1, source_target_pairs={{1,0},{2,1},{3,2},{4,3},{5,4},{6,5},{7,6},{8,7},{9,8},{10,9},{11,1... | collective-permute-start | bytes 506888 | tf_op jit(solution)/shard_map/ppermute | solution.py:18
  34.2 4.1 %collective-permute-start.8 = (f32[1,32,128]{2,1,0:T(8,128)S(1)}, f32[1,32,128]{2,1,0:T(8,128)S(1)}, u32[]{:S(2)}, u32[]{:S(2)}) collective-permute-start(f32[1,32,128]{2,1,0:T(8,128)S(1)} %get-tuple-element.82), channel_id=1, source_target_pairs={{0,32},{32,64},{64,96},{96,128},{128,160},{160,192},{192,224},{224... | collective-permute-start | bytes 49160 | tf_op jit(solution)/shard_map/ppermute | solution.py:16
  34.5 3.8 %collective-permute-start.9 = (f32[1,32,128]{2,1,0:T(8,128)S(1)}, f32[1,32,128]{2,1,0:T(8,128)S(1)}, u32[]{:S(2)}, u32[]{:S(2)}) collective-permute-start(f32[1,32,128]{2,1,0:T(8,128)S(1)} %get-tuple-element.83), channel_id=1, source_target_pairs={{32,0},{64,32},{96,64},{128,96},{160,128},{192,160},{224,192},{0,2... | collective-permute-start | bytes 49160 | tf_op jit(solution)/shard_map/ppermute | solution.py:18
  38.3 2.3 %collective-permute-start.10 = (f32[66,1,128]{2,1,0:T(1,128)S(1)}, f32[66,1,128]{2,1,0:T(1,128)S(1)}, u32[]{:S(2)}, u32[]{:S(2)}) collective-permute-start(f32[66,1,128]{2,1,0:T(1,128)S(1)} %get-tuple-element.74), channel_id=1, source_target_pairs={{0,1},{1,2},{2,3},{3,4},{4,5},{5,6},{6,7},{7,8},{8,9},{9,10},{10,1... | collective-permute-start | bytes 101384 | tf_op jit(solution)/shard_map/ppermute | solution.py:16
  39.6 6.7 %collective-permute-start.11 = (f32[66,1,128]{2,1,0:T(1,128)S(1)}, f32[66,1,128]{2,1,0:T(1,128)S(1)}, u32[]{:S(2)}, u32[]{:S(2)}) collective-permute-start(f32[66,1,128]{2,1,0:T(1,128)S(1)} %get-tuple-element.75), channel_id=1, source_target_pairs={{1,0},{2,1},{3,2},{4,3},{5,4},{6,5},{7,6},{8,7},{9,8},{10,9},{11,1... | collective-permute-start | bytes 101384 | tf_op jit(solution)/shard_map/ppermute | solution.py:18
  49.6 4.2 %collective-permute-start.12 = (f32[1,32,128]{2,1,0:T(8,128)S(1)}, f32[1,32,128]{2,1,0:T(8,128)S(1)}, u32[]{:S(2)}, u32[]{:S(2)}) collective-permute-start(f32[1,32,128]{2,1,0:T(8,128)S(1)} %get-tuple-element.80), channel_id=1, source_target_pairs={{0,32},{32,64},{64,96},{96,128},{128,160},{160,192},{192,224},{224... | collective-permute-start | bytes 49160 | tf_op jit(solution)/shard_map/ppermute | solution.py:16
  49.7 4.1 %collective-permute-start.13 = (f32[1,32,128]{2,1,0:T(8,128)S(1)}, f32[1,32,128]{2,1,0:T(8,128)S(1)}, u32[]{:S(2)}, u32[]{:S(2)}) collective-permute-start(f32[1,32,128]{2,1,0:T(8,128)S(1)} %get-tuple-element.81), channel_id=1, source_target_pairs={{32,0},{64,32},{96,64},{128,96},{160,128},{192,160},{224,192},{0,2... | collective-permute-start | bytes 49160 | tf_op jit(solution)/shard_map/ppermute | solution.py:18
  53.8 2.0 %collective-permute-start.14 = (f32[66,1,128]{2,1,0:T(1,128)S(1)}, f32[66,1,128]{2,1,0:T(1,128)S(1)}, u32[]{:S(2)}, u32[]{:S(2)}) collective-permute-start(f32[66,1,128]{2,1,0:T(1,128)S(1)} %get-tuple-element.72), channel_id=1, source_target_pairs={{0,1},{1,2},{2,3},{3,4},{4,5},{5,6},{6,7},{7,8},{8,9},{9,10},{10,1... | collective-permute-start | bytes 101384 | tf_op jit(solution)/shard_map/ppermute | solution.py:16
  54.7 6.7 %collective-permute-start.15 = (f32[66,1,128]{2,1,0:T(1,128)S(1)}, f32[66,1,128]{2,1,0:T(1,128)S(1)}, u32[]{:S(2)}, u32[]{:S(2)}) collective-permute-start(f32[66,1,128]{2,1,0:T(1,128)S(1)} %get-tuple-element.73), channel_id=1, source_target_pairs={{1,0},{2,1},{3,2},{4,3},{5,4},{6,5},{7,6},{8,7},{9,8},{10,9},{11,1... | collective-permute-start | bytes 101384 | tf_op jit(solution)/shard_map/ppermute | solution.py:18
  64.7 4.2 %collective-permute-start.16 = (f32[1,32,128]{2,1,0:T(8,128)S(1)}, f32[1,32,128]{2,1,0:T(8,128)S(1)}, u32[]{:S(2)}, u32[]{:S(2)}) collective-permute-start(f32[1,32,128]{2,1,0:T(8,128)S(1)} %get-tuple-element.78), channel_id=1, source_target_pairs={{0,32},{32,64},{64,96},{96,128},{128,160},{160,192},{192,224},{224... | collective-permute-start | bytes 49160 | tf_op jit(solution)/shard_map/ppermute | solution.py:16
  66.3 2.9 %collective-permute-start.17 = (f32[1,32,128]{2,1,0:T(8,128)S(1)}, f32[1,32,128]{2,1,0:T(8,128)S(1)}, u32[]{:S(2)}, u32[]{:S(2)}) collective-permute-start(f32[1,32,128]{2,1,0:T(8,128)S(1)} %get-tuple-element.79), channel_id=1, source_target_pairs={{32,0},{64,32},{96,64},{128,96},{160,128},{192,160},{224,192},{0,2... | collective-permute-start | bytes 49160 | tf_op jit(solution)/shard_map/ppermute | solution.py:18
  69.2 2.3 %collective-permute-start.18 = (f32[66,1,128]{2,1,0:T(1,128)S(1)}, f32[66,1,128]{2,1,0:T(1,128)S(1)}, u32[]{:S(2)}, u32[]{:S(2)}) collective-permute-start(f32[66,1,128]{2,1,0:T(1,128)S(1)} %get-tuple-element.70), channel_id=1, source_target_pairs={{0,1},{1,2},{2,3},{3,4},{4,5},{5,6},{6,7},{7,8},{8,9},{9,10},{10,1... | collective-permute-start | bytes 101384 | tf_op jit(solution)/shard_map/ppermute | solution.py:16
  70.4 6.7 %collective-permute-start.19 = (f32[66,1,128]{2,1,0:T(1,128)S(1)}, f32[66,1,128]{2,1,0:T(1,128)S(1)}, u32[]{:S(2)}, u32[]{:S(2)}) collective-permute-start(f32[66,1,128]{2,1,0:T(1,128)S(1)} %get-tuple-element.71), channel_id=1, source_target_pairs={{1,0},{2,1},{3,2},{4,3},{5,4},{6,5},{7,6},{8,7},{9,8},{10,9},{11,1... | collective-permute-start | bytes 101384 | tf_op jit(solution)/shard_map/ppermute | solution.py:18
  79.3 1.2 %copy-start.2 = (s32[64,32,128]{2,1,0:T(8,128)S(1)}, s32[64,32,128]{2,1,0:T(8,128)}, u32[]{:S(2)}) copy-start(s32[64,32,128]{2,1,0:T(8,128)} %param.8) | copy-start | bytes 3145732
  80.5 1.4 %copy-start.1 = (f32[64,32,128]{2,1,0:T(8,128)}, f32[64,32,128]{2,1,0:T(8,128)S(1)}, u32[]{:S(2)}) copy-start(f32[64,32,128]{2,1,0:T(8,128)S(1)} %fusion.22) | copy-start | bytes 3145732
  82.7 18.3 %copy-start.5 = (f32[4,32,16]{1,2,0:T(8,128)S(1)}, f32[4,32,16]{1,2,0:T(8,128)}, u32[]{:S(2)}) copy-start(f32[4,32,16]{1,2,0:T(8,128)} %constant.10.clone.1) | copy-start | bytes 24580
  82.7 17.9 %all-to-all-start = ((f32[8,1,4,32,128]{4,3,2,1,0:T(8,128)}), f32[8,1,4,32,128]{4,3,2,1,0:T(8,128)S(1)}, u32[]{:S(2)}, u32[]{:S(2)}) async-start(f32[8,1,4,32,128]{4,3,2,1,0:T(8,128)} %stack.20), calls=%async_computation | async-start | bytes 1048576 | tf_op jit(solution)/shard_map/all_to_all | solution.py:114
